TPU v7x, 32 devices: a whole 2x2x4 slice. The times are simulated.
32 devices in a mesh: wide: 4 (over z), narrow: 8 (over y, x, core).
Axes of the slice: x: 2, y: 2, z: 4, core: 2. Of those that a mesh axis runs over, the one named last changes fastest.
Arguments:
- tokens: bfloat16 [4096, 8192], P(('wide', 'narrow')), may hold values from -24 to 24, as said below
- row_cells: int32 [4096], replicated, may hold values from 0 to 4095, as said below
- documents: int32 [4096], replicated, may hold values from 0 to 3, never falling along the last dimension, each value on 1 to 3072 neighbouring positions
- query_weight: bfloat16 [8192, 512], replicated, as said below
- key_weight: bfloat16 [8192, 128], replicated, as said below
- value_weight: bfloat16 [8192, 128], replicated, may hold values from -0.0625 to 0.0625
Outputs:
- mixed: bfloat16 [4096, 512], P(('wide', 'narrow'))
Inputs may be any that keep to these rules, and one draw needn't show every extreme that they name: `row_cells`: a permutation of the cells; the rows of one device go to every device's 128 cells in equal numbers, 4 rows to each, where cells 128 * d to 128 * d + 127 are device d's. `tokens`: activations. `query_weight`: scaled by the width. `key_weight`: scaled by the width.
All inputs are finite; a program needn't handle non-finite values.
Results may differ from a plain program's by a relative error of at most 0.0063.
Values may be sent and summed in bfloat16 or wider, within the bound.
A program may use at most 128 MiB of HBM per device.

v0:
```python
import jax
import jax.numpy as jnp
from jax import lax
from jax.sharding import PartitionSpec as P

neg_large = -1e30


def joined(value, axis, join):
    pieces = jax.tree.map(lambda part: lax.all_gather(part, axis), value)
    head = jax.tree.map(lambda part: part[0], pieces)
    tail = jax.tree.map(lambda part: part[1:], pieces)
    so_far, _ = lax.scan(lambda so_far, piece: (join(so_far, piece), None), head, tail)
    return so_far


def project(rows, weights):
    return jnp.concatenate(
        [
            jnp.dot(rows, weight, preferred_element_type=jnp.float32).astype(jnp.bfloat16)
            for weight in weights
        ],
        axis=1,
    )


def shards(tokens, row_cells, documents, query_weight, key_weight, value_weight):
    rows_dev = tokens.shape[0]
    devices = lax.axis_size(("wide", "narrow"))
    own_index = lax.axis_index(("wide", "narrow"))
    narrow_count = lax.axis_size("narrow")
    wide_index = lax.axis_index("wide")
    narrow_index = lax.axis_index("narrow")
    head_size = key_weight.shape[1]
    query_width = query_weight.shape[1]
    head_count = query_width // head_size
    score_scale = head_size ** (-0.5)
    cell_table = row_cells.reshape(devices, rows_dev)
    target = cell_table // rows_dev
    ranking = jnp.argsort(
        target * rows_dev + jnp.arange(rows_dev, dtype=jnp.int32)[None, :], axis=1
    )
    sorted_cells = jnp.take_along_axis(cell_table, ranking, axis=1)
    per_pair = rows_dev // devices
    arrived_cells = sorted_cells.reshape(devices, devices, per_pair)
    arrived_slots = (
        lax.dynamic_index_in_dim(arrived_cells, own_index, 1, keepdims=False).reshape(rows_dev)
        % rows_dev
    )
    send_order = lax.dynamic_index_in_dim(ranking, own_index, 0, keepdims=False)
    placing = jnp.argsort(arrived_slots)
    weights = (query_weight, key_weight, value_weight)
    arrived_rows = lax.all_to_all(
        tokens[send_order], ("wide", "narrow"), split_axis=0, concat_axis=0, tiled=True
    )
    packed = project(arrived_rows[placing], weights)
    own_queries = packed[:, :query_width]
    own_keys = packed[:, query_width:]
    queries = lax.all_gather(own_queries, "wide", axis=0, tiled=True)
    query_count = queries.shape[0]
    local_index = jnp.arange(query_count, dtype=jnp.int32)
    query_pos = (
        local_index // rows_dev * narrow_count + narrow_index
    ) * rows_dev + local_index % rows_dev
    query_docs = documents[query_pos]
    block_rows = min(512, query_count)
    block_count = query_count // block_rows
    query_blocks = queries.reshape(block_count, block_rows, head_count, head_size)
    position_blocks = query_pos.reshape(block_count, block_rows)
    doc_blocks = query_docs.reshape(block_count, block_rows)
    key_base = wide_index * narrow_count * rows_dev
    initial = (
        jnp.full((block_count, block_rows, head_count), neg_large, jnp.float32),
        jnp.zeros((block_count, block_rows, head_count), jnp.float32),
        jnp.zeros((block_count, block_rows, head_count, head_size), jnp.float32),
    )
    key_piece = lax.all_gather(own_keys, "narrow", axis=0, tiled=True)
    piece_rows = key_piece.shape[0]
    key_pos = key_base + jnp.arange(piece_rows, dtype=jnp.int32)
    key_docs = lax.dynamic_slice_in_dim(documents, key_base, piece_rows, 0)
    keys = key_piece[:, :head_size]
    values = key_piece[:, head_size:]

    def step(carried, inputs):
        block_query, block_pos, block_doc, maxima, totals, sums = inputs
        scores = (
            jnp.einsum("qhd,kd->qhk", block_query, keys, preferred_element_type=jnp.float32)
            * score_scale
        )
        visible = (key_pos[None, :] <= block_pos[:, None]) & (
            key_docs[None, :] == block_doc[:, None]
        )
        scores = jnp.where(visible[:, None, :], scores, neg_large)
        new_max = jnp.maximum(maxima, jnp.max(scores, axis=2))
        expo = jnp.where(visible[:, None, :], jnp.exp(scores - new_max[:, :, None]), 0.0)
        factor = jnp.exp(maxima - new_max)
        new_totals = totals * factor + jnp.sum(expo, axis=2)
        product = jnp.einsum(
            "qhk,kd->qhd", expo.astype(jnp.bfloat16), values, preferred_element_type=jnp.float32
        )
        result = (new_max, new_totals, sums * factor[:, :, None] + product)
        return (carried, result)

    unused, updated = lax.scan(
        step, jnp.int32(0), (query_blocks, position_blocks, doc_blocks) + tuple(initial)
    )
    maxima = updated[0].reshape(query_count, head_count)
    totals = updated[1].reshape(query_count, head_count)
    sums = updated[2].reshape(query_count, head_count, head_size)

    def combine(first_part, second_part):
        highest = jnp.maximum(first_part[0], second_part[0])
        first_factor = jnp.exp(first_part[0] - highest)
        second_factor = jnp.exp(second_part[0] - highest)
        return (
            highest,
            first_part[1] * first_factor + second_part[1] * second_factor,
            first_part[2] * first_factor[:, :, None] + second_part[2] * second_factor[:, :, None],
        )

    merged = joined((maxima, totals, sums), "wide", combine)
    own_totals = lax.dynamic_slice_in_dim(merged[1], wide_index * rows_dev, rows_dev, 0)
    own_sums = lax.dynamic_slice_in_dim(merged[2], wide_index * rows_dev, rows_dev, 0)
    return (own_sums / own_totals[:, :, None]).reshape(rows_dev, query_width).astype(jnp.bfloat16)


def solution(mesh):
    in_specs = (P(("wide", "narrow"), None), P(), P(), P(), P(), P())
    out_specs = P(("wide", "narrow"), None)
    return jax.shard_map(shards, mesh=mesh, in_specs=in_specs, out_specs=out_specs, check_vma=False)
```

profile of v0, /device:TPU:0, one launch (start us, length us, event | category | flops | bytes accessed | tf_op | source)
XLA Modules:
  0.0 247.1 jit_solution(7424170753787183741)
XLA Ops:
  6.5 0.0 copy-start
  6.5 0.0 sort.37.cloned.1.call-start
  6.5 1.5 fusion.19
  8.0 0.6 iota.33
  8.6 0.0 sort.37.cloned.1.call-update
  8.7 4.4 %sort.37.cloned.1.call-done = (s32[32,128]{1,0:T(8,128)}, s32[32,128]{1,0:T(8,128)}) async-done(((s32[32,128]{1,0:T(8,128)}, s32[32,128]{1,0:T(8,128)}), (s32[32,128]{1,0:T(8,128)}, s32[32,128]{1,0:T(8,128)})) %sort.37.cloned.1.call-update) | async-done | bytes 32784 | tf_op jit(solution)/shard_map/jit(argsort)/sort | solution.py:40
  13.0 0.7 fusion.39
  13.7 0.0 copy-done
  13.7 3.2 %gather_fusion.1 = bf16[128,8192]{1,0:T(8,128)(2,1)} fusion(bf16[128,8192]{1,0:T(8,128)(2,1)S(1)} %copy-done, s32[1024]{0:T(1024)S(1)} %pad_clamp_fusion.1), kind=kCustom, calls=%fused_computation.1 | custom fusion | bytes 4194816 | tf_op jit(solution)/shard_map/gather | solution.py:54
  17.0 4.1 %all_to_all.8 = bf16[32,4,8192]{2,1,0:T(4,128)(2,1)} reshape(bf16[128,8192]{1,0:T(8,128)(2,1)} %gather_fusion.1) | data formatting | bytes 4194304 | tf_op jit(solution)/shard_map/all_to_all | solution.py:53
  21.1 7.4 %all-to-all-start = ((bf16[32,4,8192]{2,1,0:T(4,128)(2,1)}), bf16[32,4,8192]{2,1,0:T(4,128)(2,1)}, u32[]{:S(2)}, u32[]{:S(2)}) async-start(bf16[32,4,8192]{2,1,0:T(4,128)(2,1)} %all_to_all.8), calls=%async_computation | async-start | bytes 4194304 | tf_op jit(solution)/shard_map/all_to_all | solution.py:53
  28.5 0.0 copy-start.6
  28.5 0.0 copy-start.1
  28.5 0.0 all-gather.4.cloned.1.call-start
  28.6 0.0 dynamic-slice-start
  28.6 0.0 copy-done.2
  28.6 3.1 %gather_fusion = s32[512]{0:T(512)S(1)} fusion(s32[4096]{0:T(1024)S(1)} %copy-done.2, s32[1024]{0:T(1024)S(1)} %pad_clamp_fusion.2), kind=kCustom, calls=%fused_computation | custom fusion | bytes 6144 | tf_op jit(solution)/shard_map/gather | solution.py:65
  31.8 0.0 dynamic-slice-done
  31.8 0.5 compare_and_fusion
  32.3 0.0 copy-done.6
  32.3 0.0 copy-done.1
  32.3 25.6 %gather_fusion.3 = s32[4096]{0:T(1024)S(1)} fusion(s32[32,128]{1,0:T(8,128)S(1)} %bitcast.76, s32[4096]{0:T(1024)S(1)} %fusion.20), kind=kCustom, calls=%fused_computation.3 | custom fusion | bytes 65536 | tf_op jit(solution)/shard_map/jit(take_along_axis)/gather | solution.py:43
  58.0 0.1 copy.38
  58.1 0.1 copy.39
  58.2 0.1 reshape.225
  58.3 2.5 %sort.35 = (s32[128]{0:T(128)}, s32[128]{0:T(128)S(1)}) sort(s32[128]{0:T(128)S(1)} %and_select_fusion.2, s32[128]{0:T(128)S(1)} %iota.34), dimensions={0}, to_apply=%region_1.2 | sort | flops 896 | bytes 2048 | tf_op jit(solution)/shard_map/jit(argsort)/sort | solution.py:51
  60.9 16.5 %all-to-all-done = bf16[32,4,8192]{2,1,0:T(4,128)(2,1)} async-done(((bf16[32,4,8192]{2,1,0:T(4,128)(2,1)}), bf16[32,4,8192]{2,1,0:T(4,128)(2,1)}, u32[]{:S(2)}, u32[]{:S(2)}) %all-to-all-start) | async-done | bytes 2097184 | tf_op jit(solution)/shard_map/all_to_all | solution.py:53
  77.4 4.0 %all_to_all.10 = bf16[128,8192]{1,0:T(8,128)(2,1)} reshape(bf16[32,4,8192]{2,1,0:T(4,128)(2,1)} %all-to-all-done) | data formatting | bytes 4194304 | tf_op jit(solution)/shard_map/all_to_all | solution.py:53
  81.3 7.0 %gather_fusion.2 = bf16[128,8192]{1,0:T(8,128)(2,1)} fusion(bf16[128,8192]{1,0:T(8,128)(2,1)} %all_to_all.10, s32[1024]{0:T(1024)S(1)} %pad_clamp_fusion), kind=kCustom, calls=%fused_computation.2 | custom fusion | bytes 4194816 | tf_op jit(solution)/shard_map/gather | solution.py:56
  88.3 3.3 %convolution_convert_fusion.1 = bf16[128,128]{0,1:T(8,128)(2,1)S(1)} fusion(bf16[128,8192]{1,0:T(8,128)(2,1)} %gather_fusion.2, bf16[8192,128]{1,0:T(8,128)(2,1)} %param.13), kind=kOutput, calls=%fused_computation.24 | convolution fusion | flops 268451840 | bytes 4227072 | tf_op jit(solution)/shard_map/dot_general | solution.py:20
  91.6 0.0 copy-done.3
  91.6 0.2 copy-done.5
  91.8 1.0 convolution_convert_fusion.2
  92.8 9.9 %all_gather.16 = bf16[1024,256]{0,1:T(8,128)(2,1)S(1)} all-gather(bf16[128,256]{0,1:T(8,128)(2,1)S(1)} %pad_maximum_fusion), channel_id=1, replica_groups=mesh['wide'=4,'narrow'=8] {'narrow'}, dimensions={0}, use_global_device_ids=true | all-gather | bytes 589824 | tf_op jit(solution)/shard_map/all_gather | solution.py:77
  102.6 4.8 %convolution_convert_fusion = bf16[128,512]{1,0:T(8,128)(2,1)S(1)} fusion(bf16[128,8192]{1,0:T(8,128)(2,1)S(1)} %copy-done.3, bf16[8192,512]{1,0:T(8,128)(2,1)} %param.11), kind=kOutput, calls=%fused_computation.23 | convolution fusion | flops 1073807360 | bytes 10616832 | tf_op jit(solution)/shard_map/dot_general | solution.py:20
  107.4 16.4 %all_gather.15 = bf16[512,512]{1,0:T(8,128)(2,1)S(1)} all-gather(bf16[128,512]{1,0:T(8,128)(2,1)S(1)} %convolution_convert_fusion), channel_id=1, replica_groups=mesh['wide'=4,'narrow'=8] {'wide'}, dimensions={0}, use_global_device_ids=true | all-gather | bytes 655360 | tf_op jit(solution)/shard_map/all_gather | solution.py:59
  123.8 1.8 fusion.4
  125.6 3.0 %fusion.6 = f32[512,4]{0,1:T(4,128)S(1)} fusion(f32[512,4,1024]{2,0,1:T(8,128)S(1)} %get-tuple-element.131, f32[512,4]{0,1:T(4,128)S(1)} %broadcast_maximum_fusion, pred[512,1024]{1,0:T(8,128)(4,1)S(1)} %compare_and_fusion), kind=kLoop, calls=%fused_computation.18 | loop fusion | flops 10483712 | bytes 8929280 | tf_op jit(solution)/shard_map/while/body/eval_jaxpr/reduce_sum | solution.py:97
  128.6 3.6 %fusion.10 = f32[512,4,128]{2,0,1:T(8,128)} fusion(f32[512,4,1024]{2,0,1:T(8,128)S(1)} %get-tuple-element.131, f32[512,4]{0,1:T(4,128)S(1)} %broadcast_maximum_fusion, pred[512,1024]{1,0:T(8,128)(4,1)S(1)} %compare_and_fusion, f32[512,4]{0,1:T(4,128)S(1)} %get-tuple-element.128, bf16[1024,256]{0,1:T(8,128)(2,1)S(1)} %all_gather.16), kind=kOutput, calls=%fused_computation.22 | convolution fusion | flops 547618816 | bytes 10240000 | tf_op jit(solution)/shard_map/while/body/eval_jaxpr/qhk,kd->qhd/dot_general | solution.py:98
  132.3 0.0 all-gather.4.cloned.1.call-update
  132.3 13.1 %all-gather = f32[2048,4]{0,1:T(4,128)S(1)} all-gather(f32[512,4]{0,1:T(4,128)S(1)} %broadcast_maximum_fusion), channel_id=2, replica_groups=mesh['wide'=4,'narrow'=8] {'wide'}, dimensions={0}, use_global_device_ids=true | all-gather | bytes 40960 | tf_op jit(solution)/shard_map/all_gather | solution.py:10
  145.4 13.3 %all_gather.18 = f32[4,512,4]{1,2,0:T(4,128)S(1)} all-gather(f32[1,512,4]{1,2,0:T(4,128)S(1)} %get-tuple-element.129), channel_id=1, replica_groups=mesh['wide'=4,'narrow'=8] {'wide'}, dimensions={0}, use_global_device_ids=true | all-gather | bytes 40960 | tf_op jit(solution)/shard_map/all_gather | solution.py:10
  158.7 53.5 %all-gather.4.cloned.1.call-done = f32[2048,4,128]{2,0,1:T(8,128)} async-done(((f32[512,4,128]{2,0,1:T(8,128)}), f32[2048,4,128]{2,0,1:T(8,128)}) %all-gather.4.cloned.1.call-update) | async-done | bytes 4194320 | tf_op jit(solution)/shard_map/all_gather | solution.py:10
  212.2 1.2 slice-done
  213.4 0.7 copy.43
  214.1 3.8 %slice.51 = f32[1536,4,128]{2,0,1:T(8,128)} slice(f32[2048,4,128]{2,0,1:T(8,128)} %all-gather.4.cloned.1.call-done), slice={[512:2048], [0:4], [0:128]} | slice | bytes 6291456 | tf_op jit(solution)/shard_map/slice | solution.py:12
  217.9 21.3 %while.2 = (s32[]{:T(128)}, f32[512,4]{0,1:T(4,128)S(1)}, f32[512,4]{0,1:T(4,128)S(1)}, f32[512,4,128]{2,1,0:T(4,128)S(1)}, f32[3,512,4]{1,2,0:T(4,128)S(1)}, /*...) while((s32[]{:T(128)}, f32[512,4]{0,1:T(4,128)S(1)}, f32[512,4]{0,1:T(4,128)S(1)}, ...), condition=%wide.region_5.6_spmd, body=%wide.region_4.5_spmd.sunk | while | flops 798722 | bytes 5390457 | solution.py:13
  217.9 0.1 copy.70
  218.0 0.9 copy.71
  218.9 1.3 constant_dynamic-slice_fusion.5
  220.2 0.0 copy-done.4
  220.3 4.7 %fusion.54 = f32[512,4,128]{2,1,0:T(4,128)S(1)} fusion(f32[1,512,4,128]{3,1,0,2:T(8,128)S(1)} %constant_dynamic-slice_fusion.5, f32[512,4,128]{2,1,0:T(4,128)S(1)} %get-tuple-element.194, f32[512,4]{1,0:T(8,128)S(1)} %copy.70, f32[512,4]{1,0:T(8,128)S(1)} %copy-done.4), kind=kLoop, calls=%fused_computation.6.clone.1 | loop fusion | flops 786432 | bytes 3162112 | tf_op jit(solution)/shard_map/while/body/eval_jaxpr/add | solution.py:118
  225.0 0.1 copy.70
  225.2 0.9 copy.71
  226.0 1.3 constant_dynamic-slice_fusion.5
  227.4 0.0 copy-done.4
  227.4 4.7 %fusion.54 = f32[512,4,128]{2,1,0:T(4,128)S(1)} fusion(f32[1,512,4,128]{3,1,0,2:T(8,128)S(1)} %constant_dynamic-slice_fusion.5, f32[512,4,128]{2,1,0:T(4,128)S(1)} %get-tuple-element.194, f32[512,4]{1,0:T(8,128)S(1)} %copy.70, f32[512,4]{1,0:T(8,128)S(1)} %copy-done.4), kind=kLoop, calls=%fused_computation.6.clone.1 | loop fusion | flops 786432 | bytes 3162112 | tf_op jit(solution)/shard_map/while/body/eval_jaxpr/add | solution.py:118
  232.1 0.1 copy.70
  232.3 0.9 copy.71
  233.1 1.3 constant_dynamic-slice_fusion.5
  234.5 4.7 %fusion.54 = f32[512,4,128]{2,1,0:T(4,128)S(1)} fusion(f32[1,512,4,128]{3,1,0,2:T(8,128)S(1)} %constant_dynamic-slice_fusion.5, f32[512,4,128]{2,1,0:T(4,128)S(1)} %get-tuple-element.194, f32[512,4]{1,0:T(8,128)S(1)} %copy.70, f32[512,4]{1,0:T(8,128)S(1)} %copy-done.4), kind=kLoop, calls=%fused_computation.6.clone.1 | loop fusion | flops 786432 | bytes 3162112 | tf_op jit(solution)/shard_map/while/body/eval_jaxpr/add | solution.py:118
  239.2 0.1 copy.45
  239.3 0.2 fusion.16
  239.6 0.7 copy.65
  (31 shorter events, 0.2 us)
Async XLA Ops:
  6.5 7.2 %copy-start = (bf16[128,8192]{1,0:T(8,128)(2,1)S(1)}, bf16[128,8192]{1,0:T(8,128)(2,1)}, u32[]{:S(2)}) copy-start(bf16[128,8192]{1,0:T(8,128)(2,1)} %param.8) | copy-start | bytes 6291460
  6.5 6.5 %sort.37.cloned.1.call-start = ((), (), s32[]{:S(2)}) async-start(), calls=%async_computation.2 | async-start | bytes 98336 | tf_op jit(solution)/shard_map/jit(argsort)/sort | solution.py:40
  21.1 7.5 %copy-start.2 = (s32[4096]{0:T(1024)S(1)}, s32[4096]{0:T(1024)}, u32[]{:S(2)}) copy-start(s32[4096]{0:T(1024)} %param.10) | copy-start | bytes 49156
  21.1 56.3 %all-to-all-start = ((bf16[32,4,8192]{2,1,0:T(4,128)(2,1)}), bf16[32,4,8192]{2,1,0:T(4,128)(2,1)}, u32[]{:S(2)}, u32[]{:S(2)}) async-start(bf16[32,4,8192]{2,1,0:T(4,128)(2,1)} %all_to_all.8), calls=%async_computation | async-start | bytes 4194304 | tf_op jit(solution)/shard_map/all_to_all | solution.py:53
  28.5 3.8 %copy-start.6 = (s32[32,128]{1,0:T(8,128)S(1)}, s32[32,128]{1,0:T(8,128)}, u32[]{:S(2)}) copy-start(s32[32,128]{1,0:T(8,128)} %get-tuple-element.78) | copy-start | bytes 49156
  28.5 3.8 %copy-start.1 = (s32[4096]{0:T(1024)S(1)}, s32[4096]{0:T(1024)}, u32[]{:S(2)}) copy-start(s32[4096]{0:T(1024)} %param.9) | copy-start | bytes 49156
  28.5 183.7 %all-gather.4.cloned.1.call-start = ((), (), s32[]{:S(2)}) async-start(), calls=%async_computation.1 | async-start | bytes 5242880 | tf_op jit(solution)/shard_map/all_gather | solution.py:10
  28.6 3.2 %dynamic-slice-start = ((s32[4096]{0:T(1024)}, s32[]{:T(128)}), s32[1024]{0:T(1024)S(1)}, s32[]{:S(2)}) async-start(s32[4096]{0:T(1024)} %param.10, s32[]{:T(128)} %select_n.100), calls=%async_computation.4 | async-start | bytes 8704 | tf_op jit(solution)/shard_map/dynamic_slice | solution.py:80
  88.3 3.3 %copy-start.3 = (bf16[128,8192]{1,0:T(8,128)(2,1)S(1)}, bf16[128,8192]{1,0:T(8,128)(2,1)}, u32[]{:S(2)}) copy-start(bf16[128,8192]{1,0:T(8,128)(2,1)} %gather_fusion.2) | copy-start | bytes 6291460
  88.3 3.5 %copy-start.5 = (bf16[8192,128]{1,0:T(8,128)(2,1)S(1)}, bf16[8192,128]{1,0:T(8,128)(2,1)}, u32[]{:S(2)}) copy-start(bf16[8192,128]{1,0:T(8,128)(2,1)} %param.12) | copy-start | bytes 6291460
  212.2 1.2 slice-start
  218.9 1.3 copy-start.4
  226.0 1.3 copy-start.4
  233.1 1.3 copy-start.4
Sparse Core Ops, SparseCore 0:
  9.6 3.1 sort.39.cloned.1.call-done
  132.4 79.7 all-gather.3
  (1 shorter events, 0.0 us)
where the time goes:
time: 248 us; the launch traced here: 247 us
  waiting for transfers between devices  70 us (28%)
  local copies, waits for them, and re-layouts  66 us (27%)
  blocking collectives  52.7 us (21%)
  other arithmetic  22.7 us (9%)
  matrix products  14.4 us (6%)
  between operations  13.7 us (6%)
  starting transfers between devices  7.46 us (3%)
    all_gather x1, waiting for transfers between devices, joined(): pieces = jax.tree.map(lambda part: lax.all_gather(part, axis), value)  53.5 us
    all_gather x2, blocking collectives, joined(): pieces = jax.tree.map(lambda part: lax.all_gather(part, axis), value)  26.4 us
    gather x1, local copies, waits for them, and re-layouts, shards(): sorted_cells = jnp.take_along_axis(cell_table, ranking, axis=1)  25.6 us
    all_to_all x1, waiting for transfers between devices, shards(): lax.all_to_all(tokens[send_order], ('wide', 'narrow'), split_axis=0, conc...  16.5 us
    all_gather x1, blocking collectives, shards(): queries = lax.all_gather(own_queries, 'wide', axis=0, tiled=True)  16.4 us
    add x3, other arithmetic, combine(): first_part[2] * first_factor[:, :, None]  14.1 us
    all_gather x1, blocking collectives, shards(): key_piece = lax.all_gather(own_keys, 'narrow', axis=0, tiled=True)  9.89 us
    dot_general x3, matrix products, project(): jnp.dot(rows, weight, preferred_element_type=jnp.float32)  9.01 us
  transfers between devices with their start and end apart: 2, of which 2 were waited for; matrix products, arithmetic and copies ran while one was open for 13% of the time, Pallas kernels for 0%

commit v1 on v0

v1 whole, which is shorter than its diff:
```python
import functools
import jax
import jax.numpy as jnp
from jax import lax
from jax.experimental import pallas as pl
from jax.experimental.pallas import tpu as pltpu
from jax.sharding import PartitionSpec as P

MESH = pl.DeviceIdType.MESH
LOG2E = 1.4426950408889634
HIDDEN = -3e38
LOWEST = -1e38
CHUNKS = 8


def column_of(row, size):
    diag = lax.broadcasted_iota(jnp.int32, (size, size), 0) == lax.broadcasted_iota(
        jnp.int32, (size, size), 1
    )
    return jnp.sum(jnp.where(diag, row, 0), axis=1, keepdims=True)


def row_of(column, size):
    diag = lax.broadcasted_iota(jnp.int32, (size, size), 0) == lax.broadcasted_iota(
        jnp.int32, (size, size), 1
    )
    return jnp.sum(jnp.where(diag, column, 0), axis=0, keepdims=True)


def kernel(
    dims,
    tokens_ref, cells_ref, docs_ref, wq_ref, wk_ref, wv_ref, out_ref,
    tok, wkv, wq, kv, qsend, qrecv, query, maxima, totals, sums,
    local_sem, kv_recv, kv_send, q_send, q_recv,
):
    wide, narrow, rows, heads, size, block = dims
    devices = wide * narrow
    pair = rows // devices
    outer = narrow // 4
    depth = tok.shape[2]
    w = lax.axis_index("wide")
    p = lax.axis_index("narrow")
    me = w * narrow + p
    core = lax.rem(p, 2)
    b = lax.rem(p // 2, 2)
    a = p // 4
    flip_core = 1 - 2 * core
    flip_b = 2 - 4 * b

    def firsts(q, c):
        if outer == 2:
            qa, qb = q // 4, lax.rem(q // 2, 2)
            return q + (2 - 4 * qb) * (1 - c) + (4 - 8 * qa) * c
        return q + 2 - 4 * lax.rem(q // 2, 2)

    def second_list(q, c):
        if outer == 2:
            qa, qb = q // 4, lax.rem(q // 2, 2)
            return [q + (4 - 8 * qa) * (1 - c) + (2 - 4 * qb) * c]
        return [lax.rem(q + 4 * step, narrow) for step in range(1, outer)]

    sibling = p + flip_core
    first = firsts(p, core)
    seconds = second_list(p, core)

    barrier = pltpu.get_barrier_semaphore()

    def greet(step, carry):
        other = lax.rem(me + step, devices)
        pl.semaphore_signal(
            barrier, inc=1, device_id=(other // narrow, lax.rem(other, narrow)), device_id_type=MESH
        )
        return carry

    def chunk_copies(c):
        span = pl.ds(c * depth, depth)
        return [
            pltpu.make_async_copy(tokens_ref.at[:, span], tok.at[c], local_sem.at[0, c]),
            pltpu.make_async_copy(wk_ref.at[span, :], wkv.at[c, :, pl.ds(0, size)], local_sem.at[1, c]),
            pltpu.make_async_copy(wv_ref.at[span, :], wkv.at[c, :, pl.ds(size, size)], local_sem.at[2, c]),
        ]

    def query_copy(c):
        span = pl.ds(c * depth, depth)
        return pltpu.make_async_copy(wq_ref.at[span, :], wq.at[c], local_sem.at[3, c])

    for c in range(CHUNKS):
        for copy in chunk_copies(c):
            copy.start()
    for c in range(CHUNKS):
        query_copy(c).start()
    lax.fori_loop(1, devices, greet, 0)

    acc = jnp.zeros((rows, 2 * size), jnp.float32)
    for c in range(CHUNKS):
        for copy in chunk_copies(c):
            copy.wait()
        acc = acc + jnp.dot(tok[c], wkv[c], preferred_element_type=jnp.float32)
    kv[p, w] = acc.astype(jnp.bfloat16)

    pl.semaphore_wait(barrier, devices - 1)

    def send(q, u, to_wide, to_narrow, kind):
        pltpu.make_async_remote_copy(
            src_ref=kv.at[q, u],
            dst_ref=kv.at[q, u],
            send_sem=kv_send.at[kind],
            recv_sem=kv_recv.at[q, u],
            device_id=(to_wide, to_narrow),
            device_id_type=MESH,
        ).start()

    def arrived(q, u):
        pltpu.make_async_copy(kv.at[q, u], kv.at[q, u], kv_recv.at[q, u]).wait()

    steps = list(range(1, wide))
    steps.sort(key=lambda step: min(step, wide - step))
    send(p, w, w, first, 1)
    for other in seconds:
        send(p, w, w, other, 2)
    for step in steps:
        send(p, w, lax.rem(w + step, wide), p, 0)
    send(p, w, w, sibling, 3)

    def forward_column():
        for step in steps:
            u = lax.rem(w + wide - step, wide)
            arrived(p, u)
            send(p, u, w, first, 1)
            for other in seconds:
                send(p, u, w, other, 2)
            send(p, u, w, sibling, 3)

    def ordered():
        return [w] + [lax.rem(w + wide - step, wide) for step in steps]

    def forward_first():
        for u in ordered():
            arrived(first, u)
            for other in seconds:
                send(first, u, w, other, 2)
            send(first, u, w, sibling, 3)

    def forward_second(group):
        for u in ordered():
            arrived(group, u)
            send(group, u, w, sibling, 3)

    def take(group):
        for u in ordered():
            arrived(group, u)

    acc_q = jnp.zeros((rows, heads * size), jnp.float32)
    for c in range(CHUNKS):
        query_copy(c).wait()
        acc_q = acc_q + jnp.dot(tok[c], wq[c], preferred_element_type=jnp.float32)
    own_q = acc_q.astype(jnp.bfloat16)
    stacked = jnp.concatenate([own_q[:, h * size:(h + 1) * size] for h in range(heads)], axis=0)

    my_cells = cells_ref[pl.ds(me, 1), :]
    rank = jnp.sum((column_of(my_cells, rows) < my_cells).astype(jnp.int32), axis=0, keepdims=True)
    base_place = rank // pair * block + rank % pair
    place = jnp.concatenate([base_place + h * pair for h in range(heads)], axis=1)
    chosen = lax.broadcasted_iota(jnp.int32, (devices * block, heads * rows), 0) == place
    sorted_q = jnp.dot(
        jnp.where(chosen, 1.0, 0.0).astype(jnp.bfloat16), stacked, preferred_element_type=jnp.float32
    ).astype(jnp.bfloat16)
    qsend[...] = sorted_q.reshape(devices, block, size)

    def give(step, carry):
        other = lax.rem(me + step, devices)
        pltpu.make_async_remote_copy(
            src_ref=qsend.at[other],
            dst_ref=qrecv.at[me],
            send_sem=q_send,
            recv_sem=q_recv,
            device_id=(other // narrow, lax.rem(other, narrow)),
            device_id_type=MESH,
        ).start()
        return carry

    lax.fori_loop(1, devices, give, 0)
    qrecv[me] = qsend[me]

    forward_column()

    base = me * rows
    my_pos = base + lax.broadcasted_iota(jnp.int32, (rows, 1), 0)
    my_docs = column_of(docs_ref[pl.ds(me, 1), :], rows)

    def look(s, carry):
        before, source = carry
        before = before + (docs_ref[pl.ds(s, 1), :] < my_docs).astype(jnp.int32)
        source = source + jnp.where(cells_ref[pl.ds(s, 1), :] == my_pos, s, 0)
        return before, source

    zeros = jnp.zeros((rows, rows), jnp.int32)
    before, source = lax.fori_loop(0, devices, look, (zeros, zeros), unroll=4)
    start = jnp.sum(before, axis=1, keepdims=True)
    source = jnp.sum(source, axis=1, keepdims=True)
    earlier = (row_of(source, rows) == source) & (
        lax.broadcasted_iota(jnp.int32, (rows, rows), 1)
        < lax.broadcasted_iota(jnp.int32, (rows, rows), 0)
    )
    nth = jnp.sum(earlier.astype(jnp.int32), axis=1, keepdims=True)
    lies = source * block + nth
    lies = jnp.concatenate([lies + h * pair for h in range(heads)], axis=0)
    picked = lax.broadcasted_iota(jnp.int32, (heads * rows, devices * block), 1) == lies
    picked = jnp.where(picked, 1.0, 0.0).astype(jnp.bfloat16)

    forward_first()

    pltpu.make_async_copy(
        qrecv.at[pl.ds(0, devices - 1)], qrecv.at[pl.ds(0, devices - 1)], q_recv
    ).wait()
    query[...] = jnp.dot(
        picked, qrecv[...].reshape(devices * block, size), preferred_element_type=jnp.float32
    ).astype(jnp.bfloat16)
    maxima[...] = jnp.full(maxima.shape, LOWEST, jnp.float32)
    totals[...] = jnp.zeros(totals.shape, jnp.float32)
    sums[...] = jnp.zeros(sums.shape, jnp.float32)
    factor = size ** (-0.5) * LOG2E

    def attend(group):
        keys = kv[group, :, :, pl.ds(0, size)].reshape(wide * rows, size)
        values = kv[group, :, :, pl.ds(size, size)].reshape(wide * rows, size)
        cells = jnp.concatenate(
            [cells_ref[pl.ds(u * narrow + group, 1), :] for u in range(wide)], axis=1
        )
        seen = (cells >= start) & (cells <= my_pos)
        for h in range(heads):
            part = pl.ds(h * rows, rows)
            scores = lax.dot_general(
                query[part, :], keys, (((1,), (1,)), ((), ())), preferred_element_type=jnp.float32
            ) * factor
            scores = jnp.where(seen, scores, HIDDEN)
            old = maxima[part, :]
            top = jnp.maximum(old, jnp.max(scores, axis=1, keepdims=True))
            expo = jnp.exp2(scores - top)
            shrink = jnp.exp2(old - top)
            totals[part, :] = totals[part, :] * shrink + jnp.sum(expo, axis=1, keepdims=True)
            sums[part, :] = sums[part, :] * shrink + jnp.dot(
                expo.astype(jnp.bfloat16), values, preferred_element_type=jnp.float32
            )
            maxima[part, :] = top

    attend(p)
    for other in seconds:
        forward_second(other)
    attend(first)
    take(sibling)
    attend(sibling)
    for other in seconds:
        forward_second(firsts(other, core))
    sibling_first = firsts(sibling, 1 - core)
    take(sibling_first)
    attend(sibling_first)
    sibling_seconds = second_list(sibling, 1 - core)
    for other in seconds:
        attend(other)
    for other in sibling_seconds:
        take(other)
        attend(other)
    for other in seconds:
        attend(firsts(other, core))
    for other in sibling_seconds:
        far = firsts(other, 1 - core)
        take(far)
        attend(far)

    for h in range(heads):
        part = pl.ds(h * rows, rows)
        out_ref[:, h * size:(h + 1) * size] = (sums[part, :] / totals[part, :]).astype(jnp.bfloat16)

    spans = (kv.at[0, pl.ds(0, wide - 1)], kv.at[0], kv.at[pl.ds(0, 2 * (outer - 1))], kv.at[pl.ds(0, narrow // 2)])
    for kind, span in enumerate(spans):
        pltpu.make_async_copy(span, span, kv_send.at[kind]).wait()
    pltpu.make_async_copy(
        qsend.at[pl.ds(0, devices - 1)], qsend.at[pl.ds(0, devices - 1)], q_send
    ).wait()


def solution(mesh):
    wide, narrow = mesh.shape["wide"], mesh.shape["narrow"]
    devices = wide * narrow

    def shards(tokens, row_cells, documents, query_weight, key_weight, value_weight):
        rows, width = tokens.shape
        size = key_weight.shape[1]
        heads = query_weight.shape[1] // size
        pair = rows // devices
        block = -(-pair * heads // 16) * 16
        depth = width // CHUNKS
        dims = (wide, narrow, rows, heads, size, block)
        vmem = pl.BlockSpec(memory_space=pltpu.VMEM)
        hbm = pl.BlockSpec(memory_space=pl.ANY)
        flops = 2 * rows * width * (heads + 2) * size + 4 * rows * heads * devices * rows * size
        return pl.pallas_call(
            functools.partial(kernel, dims),
            out_shape=jax.ShapeDtypeStruct((rows, heads * size), jnp.bfloat16),
            in_specs=[hbm, vmem, vmem, hbm, hbm, hbm],
            out_specs=vmem,
            scratch_shapes=[
                pltpu.VMEM((CHUNKS, rows, depth), jnp.bfloat16),
                pltpu.VMEM((CHUNKS, depth, 2 * size), jnp.bfloat16),
                pltpu.VMEM((CHUNKS, depth, heads * size), jnp.bfloat16),
                pltpu.VMEM((narrow, wide, rows, 2 * size), jnp.bfloat16),
                pltpu.VMEM((devices, block, size), jnp.bfloat16),
                pltpu.VMEM((devices, block, size), jnp.bfloat16),
                pltpu.VMEM((heads * rows, size), jnp.bfloat16),
                pltpu.VMEM((heads * rows, 1), jnp.float32),
                pltpu.VMEM((heads * rows, 1), jnp.float32),
                pltpu.VMEM((heads * rows, size), jnp.float32),
                pltpu.SemaphoreType.DMA((4, CHUNKS)),
                pltpu.SemaphoreType.DMA((narrow, wide)),
                pltpu.SemaphoreType.DMA((4,)),
                pltpu.SemaphoreType.DMA,
                pltpu.SemaphoreType.DMA,
            ],
            compiler_params=pltpu.CompilerParams(
                collective_id=0, has_side_effects=True, vmem_limit_bytes=56 * 1024 * 1024
            ),
            cost_estimate=pl.CostEstimate(
                flops=flops, bytes_accessed=16 * 1024 * 1024, transcendentals=rows * heads * devices * rows
            ),
        )(
            tokens,
            row_cells.reshape(devices, rows),
            documents.reshape(devices, rows),
            query_weight,
            key_weight,
            value_weight,
        )

    in_specs = (P(("wide", "narrow"), None), P(), P(), P(), P(), P())
    return jax.shard_map(
        shards, mesh=mesh, in_specs=in_specs, out_specs=P(("wide", "narrow"), None), check_vma=False
    )
```

time: 248 us -> 36.3 us (0.15)
  waiting for transfers between devices: 70 us -> 0 us
  local copies, waits for them, and re-layouts: 66 us -> 1.57 us
  blocking collectives: 52.7 us -> 0 us
  Pallas kernels: 0 us -> 34.4 us
  other arithmetic: 22.7 us -> 0 us
  matrix products: 14.4 us -> 0 us
  between operations: 13.7 us -> 0.01 us
  starting transfers between devices: 7.46 us -> 0 us
    all_gather x1 -> x0, waiting for transfers between devices: 53.5 us -> none  [joined(): pieces = jax.tree.map(lambda part: lax.all_gather(part, axis), value)]
    all_gather x4 -> x0, blocking collectives: 52.7 us -> none  [the longest x2 26.4 us: joined(): pieces = jax.tree.map(lambda part: lax.all_gather(part, axis), value)]
    gather x4 -> x0, local copies, waits for them, and re-layouts: 38.9 us -> none  [the longest x1 25.6 us: shards(): sorted_cells = jnp.take_along_axis(cell_table, ranking, axis=1)]
    pallas_call x0 -> x1, Pallas kernels: none -> 34.4 us  [shards(): pl.pallas_call(functools.partial(kernel, dims), out_shape=jax.ShapeDtypeS...]
    all_to_all x1 -> x0, waiting for transfers between devices: 16.5 us -> none  [shards(): lax.all_to_all(tokens[send_order], ('wide', 'narrow'), split_axis=0, conc...]
    add x9 -> x0, other arithmetic: 15.7 us -> none  [the longest x3 14.1 us: combine(): first_part[2] * first_factor[:, :, None]]
    dot_general x5 -> x0, matrix products: 14.4 us -> none  [the longest x3 9.01 us: project(): jnp.dot(rows, weight, preferred_element_type=jnp.float32)]
    all_to_all x2 -> x0, local copies, waits for them, and re-layouts: 8.06 us -> none  [shards(): lax.all_to_all(tokens[send_order], ('wide', 'narrow'), split_axis=0, conc...]
  transfers between devices with their start and end apart: 2 -> 0, of which waited for: 2 -> 0; matrix products, arithmetic and copies ran while one was open for 13% -> 0% of each run, Pallas kernels for 0% -> 0%
where the time goes in v1:
time: 36.3 us; the launch traced here: 36 us
  Pallas kernels  34.4 us (95%)
  local copies, waits for them, and re-layouts  1.57 us (4%)
    pallas_call x1, Pallas kernels, shards(): pl.pallas_call(functools.partial(kernel, dims), out_shape=jax.ShapeDtypeS...  34.4 us
    unnamed x1, local copies, waits for them, and re-layouts  1.57 us

profile of v1, /device:TPU:0, one launch (start us, length us, event | category | flops | bytes accessed | tf_op | source)
XLA Modules:
  0.0 36.0 jit_solution(4903587684113096085)
XLA Ops:
  0.0 34.4 %shard_map.64 = bf16[128,512]{1,0:T(8,128)(2,1)} custom-call(bf16[128,8192]{1,0:T(8,128)(2,1)} %tokens_ref.1, s32[32,128]{1,0:T(8,128)} %bitcast.2, s32[32,128]{1,0:T(8,128)} %bitcast.3, bf16[8192,512]{1,0:T(8,128)(2,1)} %wq_ref.1, bf16[8192,128]{1,0:T(8,128)(2,1)} %wk_ref.1, bf16[8192,128]{1,0:T(8,128)(2,1)} %wv_ref.1), custom_call_target="tpu_custom_call" | custom-call | flops 2684354560 | bytes 16777216 | tf_op jit(solution)/shard_map/pallas_call | solution.py:298
  34.4 1.6 %copy.8 = bf16[128,512]{1,0:T(8,128)(2,1)} copy(bf16[128,512]{1,0:T(8,128)(2,1)} %shard_map.64) | data formatting | bytes 262144

commit v2 on v1

--- a/solution.py
+++ b/solution.py
@@ -30,7 +30,7 @@
 def kernel(
     dims,
     tokens_ref, cells_ref, docs_ref, wq_ref, wk_ref, wv_ref, out_ref,
-    tok, wkv, wq, kv, qsend, qrecv, query, maxima, totals, sums,
+    tok, wkv, wq, kv, qsend, qmid, qrecv, query, maxima, sums,
     local_sem, kv_recv, kv_send, q_send, q_recv,
 ):
     wide, narrow, rows, heads, size, block = dims
@@ -65,12 +65,15 @@
 
     barrier = pltpu.get_barrier_semaphore()
 
-    def greet(step, carry):
-        other = lax.rem(me + step, devices)
+    def greet(to_wide, to_narrow):
         pl.semaphore_signal(
-            barrier, inc=1, device_id=(other // narrow, lax.rem(other, narrow)), device_id_type=MESH
-        )
-        return carry
+            barrier, inc=1, device_id=(to_wide, to_narrow), device_id_type=MESH
+        )
+
+    for step in range(1, narrow):
+        greet(w, lax.rem(p + step, narrow))
+    for step in range(1, wide):
+        greet(lax.rem(w + step, wide), p)
 
     def chunk_copies(c):
         span = pl.ds(c * depth, depth)
@@ -89,7 +92,33 @@
             copy.start()
     for c in range(CHUNKS):
         query_copy(c).start()
-    lax.fori_loop(1, devices, greet, 0)
+
+    my_cells = cells_ref[pl.ds(me, 1), :]
+    rank = jnp.sum((column_of(my_cells, rows) < my_cells).astype(jnp.int32), axis=0, keepdims=True)
+    base_place = rank // pair * block + rank % pair
+    place = jnp.concatenate([base_place + h * pair for h in range(heads)], axis=1)
+
+    base = me * rows
+    my_pos = base + lax.broadcasted_iota(jnp.int32, (rows, 1), 0)
+    my_docs = column_of(docs_ref[pl.ds(me, 1), :], rows)
+
+    def look(s, carry):
+        before, source = carry
+        before = before + (docs_ref[pl.ds(s, 1), :] < my_docs).astype(jnp.int32)
+        source = source + jnp.where(cells_ref[pl.ds(s, 1), :] == my_pos, s, 0)
+        return before, source
+
+    zeros = jnp.zeros((rows, rows), jnp.int32)
+    before, source = lax.fori_loop(0, devices, look, (zeros, zeros), unroll=4)
+    start = jnp.sum(before, axis=1, keepdims=True)
+    source = jnp.sum(source, axis=1, keepdims=True)
+    earlier = (row_of(source, rows) == source) & (
+        lax.broadcasted_iota(jnp.int32, (rows, rows), 1)
+        < lax.broadcasted_iota(jnp.int32, (rows, rows), 0)
+    )
+    nth = jnp.sum(earlier.astype(jnp.int32), axis=1, keepdims=True)
+    lies = (source % narrow * wide + source // narrow) * block + nth
+    lies = jnp.concatenate([lies + h * pair for h in range(heads)], axis=0)
 
     acc = jnp.zeros((rows, 2 * size), jnp.float32)
     for c in range(CHUNKS):
@@ -98,7 +127,7 @@
         acc = acc + jnp.dot(tok[c], wkv[c], preferred_element_type=jnp.float32)
     kv[p, w] = acc.astype(jnp.bfloat16)
 
-    pl.semaphore_wait(barrier, devices - 1)
+    pl.semaphore_wait(barrier, narrow + wide - 2)
 
     def send(q, u, to_wide, to_narrow, kind):
         pltpu.make_async_remote_copy(
@@ -122,102 +151,88 @@
         send(p, w, lax.rem(w + step, wide), p, 0)
     send(p, w, w, sibling, 3)
 
-    def forward_column():
-        for step in steps:
-            u = lax.rem(w + wide - step, wide)
-            arrived(p, u)
-            send(p, u, w, first, 1)
-            for other in seconds:
-                send(p, u, w, other, 2)
-            send(p, u, w, sibling, 3)
-
-    def ordered():
-        return [w] + [lax.rem(w + wide - step, wide) for step in steps]
-
-    def forward_first():
-        for u in ordered():
-            arrived(first, u)
-            for other in seconds:
-                send(first, u, w, other, 2)
-            send(first, u, w, sibling, 3)
+    sources = [w] + [lax.rem(w + wide - step, wide) for step in steps]
+
+    def pass_column(u):
+        arrived(p, u)
+        send(p, u, w, first, 1)
+        for other in seconds:
+            send(p, u, w, other, 2)
+        send(p, u, w, sibling, 3)
+
+    def pass_first(u):
+        arrived(first, u)
+        for other in seconds:
+            send(first, u, w, other, 2)
+        send(first, u, w, sibling, 3)
 
     def forward_second(group):
-        for u in ordered():
+        for u in sources:
             arrived(group, u)
             send(group, u, w, sibling, 3)
 
     def take(group):
-        for u in ordered():
+        for u in sources:
             arrived(group, u)
 
     acc_q = jnp.zeros((rows, heads * size), jnp.float32)
     for c in range(CHUNKS):
         query_copy(c).wait()
         acc_q = acc_q + jnp.dot(tok[c], wq[c], preferred_element_type=jnp.float32)
+        if c == CHUNKS // 2:
+            for u in sources[1:3]:
+                pass_column(u)
+            pass_first(w)
     own_q = acc_q.astype(jnp.bfloat16)
     stacked = jnp.concatenate([own_q[:, h * size:(h + 1) * size] for h in range(heads)], axis=0)
 
-    my_cells = cells_ref[pl.ds(me, 1), :]
-    rank = jnp.sum((column_of(my_cells, rows) < my_cells).astype(jnp.int32), axis=0, keepdims=True)
-    base_place = rank // pair * block + rank % pair
-    place = jnp.concatenate([base_place + h * pair for h in range(heads)], axis=1)
     chosen = lax.broadcasted_iota(jnp.int32, (devices * block, heads * rows), 0) == place
     sorted_q = jnp.dot(
         jnp.where(chosen, 1.0, 0.0).astype(jnp.bfloat16), stacked, preferred_element_type=jnp.float32
     ).astype(jnp.bfloat16)
-    qsend[...] = sorted_q.reshape(devices, block, size)
-
-    def give(step, carry):
-        other = lax.rem(me + step, devices)
+    qsend[...] = sorted_q.reshape(wide, narrow, block, size)
+    for step in steps:
+        other = lax.rem(w + step, wide)
         pltpu.make_async_remote_copy(
             src_ref=qsend.at[other],
-            dst_ref=qrecv.at[me],
-            send_sem=q_send,
-            recv_sem=q_recv,
-            device_id=(other // narrow, lax.rem(other, narrow)),
+            dst_ref=qmid.at[w],
+            send_sem=q_send.at[0],
+            recv_sem=q_recv.at[0],
+            device_id=(other, p),
             device_id_type=MESH,
         ).start()
-        return carry
-
-    lax.fori_loop(1, devices, give, 0)
-    qrecv[me] = qsend[me]
-
-    forward_column()
-
-    base = me * rows
-    my_pos = base + lax.broadcasted_iota(jnp.int32, (rows, 1), 0)
-    my_docs = column_of(docs_ref[pl.ds(me, 1), :], rows)
-
-    def look(s, carry):
-        before, source = carry
-        before = before + (docs_ref[pl.ds(s, 1), :] < my_docs).astype(jnp.int32)
-        source = source + jnp.where(cells_ref[pl.ds(s, 1), :] == my_pos, s, 0)
-        return before, source
-
-    zeros = jnp.zeros((rows, rows), jnp.int32)
-    before, source = lax.fori_loop(0, devices, look, (zeros, zeros), unroll=4)
-    start = jnp.sum(before, axis=1, keepdims=True)
-    source = jnp.sum(source, axis=1, keepdims=True)
-    earlier = (row_of(source, rows) == source) & (
-        lax.broadcasted_iota(jnp.int32, (rows, rows), 1)
-        < lax.broadcasted_iota(jnp.int32, (rows, rows), 0)
-    )
-    nth = jnp.sum(earlier.astype(jnp.int32), axis=1, keepdims=True)
-    lies = source * block + nth
-    lies = jnp.concatenate([lies + h * pair for h in range(heads)], axis=0)
+    qmid[w] = qsend[w]
+
+    for u in sources[3:]:
+        pass_column(u)
+    for u in sources[1:3]:
+        pass_first(u)
+
+    waited = qmid.at[pl.ds(0, wide - 1)]
+    pltpu.make_async_copy(waited, waited, q_recv.at[0]).wait()
+    for step in range(1, narrow):
+        other = lax.rem(p + step, narrow)
+        pltpu.make_async_remote_copy(
+            src_ref=qmid.at[:, other],
+            dst_ref=qrecv.at[p],
+            send_sem=q_send.at[1],
+            recv_sem=q_recv.at[1],
+            device_id=(w, other),
+            device_id_type=MESH,
+        ).start()
+    qrecv[p] = qmid[:, pl.ds(p, 1)].reshape(wide, block, size)
+    for u in sources[3:]:
+        pass_first(u)
+
     picked = lax.broadcasted_iota(jnp.int32, (heads * rows, devices * block), 1) == lies
     picked = jnp.where(picked, 1.0, 0.0).astype(jnp.bfloat16)
 
-    forward_first()
-
-    pltpu.make_async_copy(
-        qrecv.at[pl.ds(0, devices - 1)], qrecv.at[pl.ds(0, devices - 1)], q_recv
-    ).wait()
+    waited = qrecv.at[pl.ds(0, narrow - 1)]
+    pltpu.make_async_copy(waited, waited, q_recv.at[1]).wait()
     query[...] = jnp.dot(
         picked, qrecv[...].reshape(devices * block, size), preferred_element_type=jnp.float32
     ).astype(jnp.bfloat16)
     maxima[...] = jnp.full(maxima.shape, LOWEST, jnp.float32)
-    totals[...] = jnp.zeros(totals.shape, jnp.float32)
     sums[...] = jnp.zeros(sums.shape, jnp.float32)
     factor = size ** (-0.5) * LOG2E
 
@@ -228,21 +243,25 @@
             [cells_ref[pl.ds(u * narrow + group, 1), :] for u in range(wide)], axis=1
         )
         seen = (cells >= start) & (cells <= my_pos)
+        wider = jnp.concatenate([values, jnp.ones_like(values)], axis=1)
+        scores = lax.dot_general(
+            query[...], keys, (((1,), (1,)), ((), ())), preferred_element_type=jnp.float32
+        )
+        expos, shrinks = [], []
         for h in range(heads):
             part = pl.ds(h * rows, rows)
-            scores = lax.dot_general(
-                query[part, :], keys, (((1,), (1,)), ((), ())), preferred_element_type=jnp.float32
-            ) * factor
-            scores = jnp.where(seen, scores, HIDDEN)
+            shown = jnp.where(seen, scores[h * rows:(h + 1) * rows] * factor, HIDDEN)
             old = maxima[part, :]
-            top = jnp.maximum(old, jnp.max(scores, axis=1, keepdims=True))
-            expo = jnp.exp2(scores - top)
-            shrink = jnp.exp2(old - top)
-            totals[part, :] = totals[part, :] * shrink + jnp.sum(expo, axis=1, keepdims=True)
-            sums[part, :] = sums[part, :] * shrink + jnp.dot(
-                expo.astype(jnp.bfloat16), values, preferred_element_type=jnp.float32
-            )
+            top = jnp.maximum(old, jnp.max(shown, axis=1, keepdims=True))
+            expos.append(jnp.exp2(shown - top).astype(jnp.bfloat16))
+            shrinks.append(jnp.exp2(old - top))
             maxima[part, :] = top
+        product = jnp.dot(
+            jnp.concatenate(expos, axis=0), wider, preferred_element_type=jnp.float32
+        )
+        for h in range(heads):
+            part = pl.ds(h * rows, rows)
+            sums[part, :] = sums[part, :] * shrinks[h] + product[h * rows:(h + 1) * rows]
 
     attend(p)
     for other in seconds:
@@ -270,14 +289,15 @@
 
     for h in range(heads):
         part = pl.ds(h * rows, rows)
-        out_ref[:, h * size:(h + 1) * size] = (sums[part, :] / totals[part, :]).astype(jnp.bfloat16)
+        out_ref[:, h * size:(h + 1) * size] = (
+            sums[part, pl.ds(0, size)] / sums[part, pl.ds(size, size)]
+        ).astype(jnp.bfloat16)
 
     spans = (kv.at[0, pl.ds(0, wide - 1)], kv.at[0], kv.at[pl.ds(0, 2 * (outer - 1))], kv.at[pl.ds(0, narrow // 2)])
     for kind, span in enumerate(spans):
         pltpu.make_async_copy(span, span, kv_send.at[kind]).wait()
-    pltpu.make_async_copy(
-        qsend.at[pl.ds(0, devices - 1)], qsend.at[pl.ds(0, devices - 1)], q_send
-    ).wait()
+    for kind, span in enumerate((qsend.at[pl.ds(0, wide - 1)], qrecv.at[pl.ds(0, narrow - 1)])):
+        pltpu.make_async_copy(span, span, q_send.at[kind]).wait()
 
 
 def solution(mesh):
@@ -305,17 +325,17 @@
                 pltpu.VMEM((CHUNKS, depth, 2 * size), jnp.bfloat16),
                 pltpu.VMEM((CHUNKS, depth, heads * size), jnp.bfloat16),
                 pltpu.VMEM((narrow, wide, rows, 2 * size), jnp.bfloat16),
-                pltpu.VMEM((devices, block, size), jnp.bfloat16),
-                pltpu.VMEM((devices, block, size), jnp.bfloat16),
+                pltpu.VMEM((wide, narrow, block, size), jnp.bfloat16),
+                pltpu.VMEM((wide, narrow, block, size), jnp.bfloat16),
+                pltpu.VMEM((narrow, wide, block, size), jnp.bfloat16),
                 pltpu.VMEM((heads * rows, size), jnp.bfloat16),
                 pltpu.VMEM((heads * rows, 1), jnp.float32),
-                pltpu.VMEM((heads * rows, 1), jnp.float32),
-                pltpu.VMEM((heads * rows, size), jnp.float32),
+                pltpu.VMEM((heads * rows, 2 * size), jnp.float32),
                 pltpu.SemaphoreType.DMA((4, CHUNKS)),
                 pltpu.SemaphoreType.DMA((narrow, wide)),
                 pltpu.SemaphoreType.DMA((4,)),
-                pltpu.SemaphoreType.DMA,
-                pltpu.SemaphoreType.DMA,
+                pltpu.SemaphoreType.DMA((2,)),
+                pltpu.SemaphoreType.DMA((2,)),
             ],
             compiler_params=pltpu.CompilerParams(
                 collective_id=0, has_side_effects=True, vmem_limit_bytes=56 * 1024 * 1024

time: 36.3 us -> 33.5 us (0.923)
  Pallas kernels: 34.4 us -> 31.6 us
    pallas_call x1, Pallas kernels: 34.4 us -> 31.6 us  [shards(): pl.pallas_call(functools.partial(kernel, dims), out_shape=jax.ShapeDtypeS...]
where the time goes in v2:
time: 33.5 us; the launch traced here: 33.2 us
  Pallas kernels  31.6 us (94%)
  local copies, waits for them, and re-layouts  1.57 us (5%)
    pallas_call x1, Pallas kernels, shards(): pl.pallas_call(functools.partial(kernel, dims), out_shape=jax.ShapeDtypeS...  31.6 us
    unnamed x1, local copies, waits for them, and re-layouts  1.57 us

profile of v2, /device:TPU:0, one launch (start us, length us, event | category | flops | bytes accessed | tf_op | source)
XLA Modules:
  0.0 33.2 jit_solution(3876701247918620497)
XLA Ops:
  0.0 31.6 %shard_map.64 = bf16[128,512]{1,0:T(8,128)(2,1)} custom-call(bf16[128,8192]{1,0:T(8,128)(2,1)} %tokens_ref.1, s32[32,128]{1,0:T(8,128)} %bitcast.2, s32[32,128]{1,0:T(8,128)} %bitcast.3, bf16[8192,512]{1,0:T(8,128)(2,1)} %wq_ref.1, bf16[8192,128]{1,0:T(8,128)(2,1)} %wk_ref.1, bf16[8192,128]{1,0:T(8,128)(2,1)} %wv_ref.1), custom_call_target="tpu_custom_call" | custom-call | flops 2684354560 | bytes 16777216 | tf_op jit(solution)/shard_map/pallas_call | solution.py:318
  31.6 1.6 %copy.8 = bf16[128,512]{1,0:T(8,128)(2,1)} copy(bf16[128,512]{1,0:T(8,128)(2,1)} %shard_map.64) | data formatting | bytes 262144

commit v3 on v2

--- a/solution.py
+++ b/solution.py
@@ -227,6 +227,9 @@
     picked = lax.broadcasted_iota(jnp.int32, (heads * rows, devices * block), 1) == lies
     picked = jnp.where(picked, 1.0, 0.0).astype(jnp.bfloat16)
 
+    for other in seconds:
+        forward_second(other)
+
     waited = qrecv.at[pl.ds(0, narrow - 1)]
     pltpu.make_async_copy(waited, waited, q_recv.at[1]).wait()
     query[...] = jnp.dot(
@@ -265,12 +268,10 @@
 
     attend(p)
     for other in seconds:
-        forward_second(other)
+        forward_second(firsts(other, core))
     attend(first)
     take(sibling)
     attend(sibling)
-    for other in seconds:
-        forward_second(firsts(other, core))
     sibling_first = firsts(sibling, 1 - core)
     take(sibling_first)
     attend(sibling_first)

time: 33.5 us -> 33.5 us (level)
  no operation moved by 1% of the time
where the time goes in v3:
time: 33.5 us; the launch traced here: 33.1 us
  Pallas kernels  31.6 us (94%)
  local copies, waits for them, and re-layouts  1.57 us (5%)
    pallas_call x1, Pallas kernels, shards(): pl.pallas_call(functools.partial(kernel, dims), out_shape=jax.ShapeDtypeS...  31.6 us
    unnamed x1, local copies, waits for them, and re-layouts  1.57 us

profile of v3, /device:TPU:0, one launch (start us, length us, event | category | flops | bytes accessed | tf_op | source)
XLA Modules:
  0.0 33.1 jit_solution(16472098240212436220)
XLA Ops:
  0.0 31.6 %shard_map.64 = bf16[128,512]{1,0:T(8,128)(2,1)} custom-call(bf16[128,8192]{1,0:T(8,128)(2,1)} %tokens_ref.1, s32[32,128]{1,0:T(8,128)} %bitcast.2, s32[32,128]{1,0:T(8,128)} %bitcast.3, bf16[8192,512]{1,0:T(8,128)(2,1)} %wq_ref.1, bf16[8192,128]{1,0:T(8,128)(2,1)} %wk_ref.1, bf16[8192,128]{1,0:T(8,128)(2,1)} %wv_ref.1), custom_call_target="tpu_custom_call" | custom-call | flops 2684354560 | bytes 16777216 | tf_op jit(solution)/shard_map/pallas_call | solution.py:319
  31.6 1.6 %copy.8 = bf16[128,512]{1,0:T(8,128)(2,1)} copy(bf16[128,512]{1,0:T(8,128)(2,1)} %shard_map.64) | data formatting | bytes 262144
